TPU v7x, 512 devices: a whole 4x4x16 slice. The times are simulated.
512 devices in a mesh: pipe: 4 (over y), seq: 16 (over z), tensor: 8 (over x, core).
Axes of the slice: x: 4, y: 4, z: 16, core: 2. Of those that a mesh axis runs over, the one named last changes fastest.
Arguments:
- layer_input: bfloat16 [4, 2048, 8192], P('pipe', 'seq', 'tensor'), may hold values from -320 to 320
- conv_out: bfloat16 [4, 2048, 8192], P('pipe', 'seq', 'tensor'), may hold values from -8 to 8
- act_grad: bfloat16 [4, 2048, 8192], P('pipe', 'seq', 'tensor'), may hold values from -6 to 6
- conv_kernel: bfloat16 [4, 4, 8192], P('pipe', None, 'tensor'), may hold values from -3 to 3
- in_proj: bfloat16 [4, 8192, 8192], P('pipe', 'seq', 'tensor'), may hold values from -0.0625 to 0.0625
- sketch_matrix: bfloat16 [4, 8192, 512], P('pipe', 'tensor'), may hold values from -0.0625 to 0.0625
Outputs:
- passed_grad: bfloat16 [4, 2048, 8192], P('pipe', 'tensor', 'seq')
- basis: bfloat16 [4, 8192, 512], P('pipe', 'tensor')
All inputs are finite; a program needn't handle non-finite values.
Results may differ from a plain program's by a relative error of at most 0.017.
Values may be sent and summed in bfloat16 or wider, within the bound.
No kernel may reach another device: no remote copies, remote signals or barrier semaphores. Data moves between devices by JAX's collectives and lax.ppermute only.
A program may use at most 64 MiB of HBM per device.

v0:
```python
import math
import jax
import jax.numpy as jnp
from jax import lax
from jax.sharding import PartitionSpec as P

D = 8192


def passed_along(block, axis, distance):
    devices = range(lax.axis_size(axis))
    route = [(i - distance, i) for i in devices if i - distance in devices]
    return lax.ppermute(block, axis, route)


def shifted(value, axis, by):
    count = lax.axis_size(axis)
    return lax.ppermute(value, axis, [(i, (i + by) % count) for i in range(count)])


def finish_basis(sketch, gram):
    low = jnp.linalg.cholesky(gram)
    ortho_t = lax.linalg.triangular_solve(low, sketch.T, left_side=True, lower=True)
    return (ortho_t.T * math.sqrt(D)).astype(jnp.bfloat16)


def local(layer_input, conv_out, act_grad, conv_kernel, in_proj, sketch_matrix):
    acts = layer_input[0]
    kernel = conv_kernel[0]
    weights = in_proj[0]
    test_matrix = sketch_matrix[0]
    tok_rows = acts.shape[0]
    taps = kernel.shape[0]
    pval = conv_out[0].astype(jnp.float32)
    sig = jax.nn.sigmoid(pval)
    pre_grad = act_grad[0].astype(jnp.float32) * sig * (1.0 + pval * (1.0 - sig))
    ahead = passed_along(pre_grad[: taps - 1], "seq", -1)
    extended = jnp.concatenate([pre_grad, ahead], axis=0)
    total = jnp.zeros(pre_grad.shape, jnp.float32)
    for tap in range(taps):
        total = total + kernel[tap].astype(jnp.float32) * extended[tap : tap + tok_rows]
    in_grad = total.astype(jnp.bfloat16)
    partial_grad = lax.dot_general(
        lax.all_gather(in_grad, "seq", axis=0, tiled=True),
        weights,
        (((1,), (1,)), ((), ())),
        preferred_element_type=jnp.float32,
    )
    input_grad = lax.psum_scatter(
        partial_grad.astype(jnp.bfloat16), "tensor", scatter_dimension=0, tiled=True
    )
    passed = shifted(input_grad, "pipe", -1)
    row_terms = jnp.dot(in_grad, test_matrix, preferred_element_type=jnp.float32)
    sketch_rows = lax.psum(row_terms, "tensor").astype(jnp.bfloat16)
    sketch_part = lax.dot_general(
        acts, sketch_rows, (((0,), (0,)), ((), ())), preferred_element_type=jnp.float32
    )
    sketch = lax.psum(sketch_part, "seq")
    gram_part = jnp.dot(sketch.T, sketch, precision=lax.Precision.HIGHEST)
    gram = lax.psum(gram_part, "tensor")
    basis = finish_basis(sketch, gram)
    return (passed[None], basis[None])


def solution(mesh):
    placed = (
        P("pipe", "seq", "tensor"),
        P("pipe", "seq", "tensor"),
        P("pipe", "seq", "tensor"),
        P("pipe", None, "tensor"),
        P("pipe", "seq", "tensor"),
        P("pipe", "tensor", None),
    )
    return jax.shard_map(
        local,
        mesh=mesh,
        in_specs=placed,
        out_specs=(P("pipe", "tensor", "seq"), P("pipe", "tensor", None)),
        check_vma=False,
    )
```

profile of v0, /device:TPU:26, one launch (start us, length us, event | category | flops | bytes accessed | tf_op | source)
XLA Modules:
  0.0 470.1 jit_solution(17740369245081746752)
XLA Ops:
  7.2 1.4 fusion.30
  8.7 1.3 collective-permute-start
  10.0 0.9 slice_convert_fusion.3
  10.8 3.5 collective-permute-done
  14.3 0.2 fusion.22
  14.6 0.3 fusion.15
  14.9 24.3 %all-reduce.8 = bf16[128,512]{1,0:T(8,128)(2,1)S(1)} all-reduce(f32[128,512]{1,0:T(8,128)S(1)} %fusion.15), channel_id=1, replica_groups=mesh['pipe'=4,'seq'=16,'tensor'=8] {'tensor'}, use_global_device_ids=true, to_apply=%region_1.0 | all-reduce | flops 65536 | bytes 393216 | tf_op jit(solution)/shard_map/psum | solution.py:54
  39.2 1.8 convolution_bitcast_fusion
  41.0 149.0 %all-reduce.5.cloned.1.call-done = f32[1024,512]{0,1:T(8,128)} async-done(((f32[1024,512]{0,1:T(8,128)}), f32[1024,512]{0,1:T(8,128)}) %all-reduce.5.cloned.1.call-update) | async-done | bytes 2097168 | tf_op jit(solution)/shard_map/psum | solution.py:58
  190.0 6.7 %fusion.56 = f32[512,512]{0,1:T(8,128)} fusion(f32[1024,512]{0,1:T(8,128)} %all-reduce.5.cloned.1.call-done), kind=kOutput, calls=%fused_computation.103 | convolution fusion | flops 3221225472 | bytes 3145728 | tf_op jit(solution)/shard_map/dot_general | solution.py:59
  196.8 0.7 all-gather.2.cloned.1.call-update
  197.5 0.5 reduce-scatter.2.cloned.1.call-start
  198.0 70.5 %all-reduce.7.cloned.1.call-done = f32[512,512]{0,1:T(8,128)} async-done(((f32[512,512]{0,1:T(8,128)}), f32[512,512]{0,1:T(8,128)}) %all-reduce.7.cloned.1.call-update) | async-done | bytes 1048592 | tf_op jit(solution)/shard_map/psum | solution.py:60
  268.5 1.6 copy.9
  270.2 0.2 fusion.14
  270.4 1.0 copy-done.7
  271.4 11.7 %cholesky.104 = f32[128,128]{1,0:T(8,128)S(1)} custom-call(f32[128,128]{1,0:T(8,128)S(1)} %cholesky.266), custom_call_target="Cholesky" | custom-call | tf_op jit(solution)/shard_map/jit(cholesky)/cholesky | solution.py:22
  283.1 0.1 cholesky.224
  283.3 9.8 %custom-call.30 = f32[1,128,128]{1,2,0:T(8,128)S(1)} custom-call(f32[1,128,128]{2,1,0:T(8,128)S(1)} %get-tuple-element.31), custom_call_target="InvertDiagBlocksLowerTriangular" | custom-call | tf_op jit(solution)/shard_map/jit(cholesky)/cholesky | solution.py:22
  293.1 1.2 constant_dynamic-update-slice_fusion.3
  294.4 1.3 convolution_subtract_fusion.2
  295.6 11.7 %cholesky.217 = f32[128,128]{1,0:T(8,128)S(1)} custom-call(f32[128,128]{1,0:T(8,128)S(1)} %cholesky.270), custom_call_target="Cholesky" | custom-call | tf_op jit(solution)/shard_map/jit(cholesky)/cholesky | solution.py:22
  307.4 10.0 %custom-call.31 = f32[1,128,128]{1,2,0:T(8,128)S(1)} custom-call(f32[1,128,128]{2,1,0:T(8,128)S(1)} %get-tuple-element.28), custom_call_target="InvertDiagBlocksLowerTriangular" | custom-call | tf_op jit(solution)/shard_map/jit(cholesky)/cholesky | solution.py:22
  317.3 0.3 convolution_dynamic-update-slice_fusion
  317.6 1.4 convolution_subtract_fusion.3
  319.1 11.7 %cholesky.238 = f32[128,128]{1,0:T(8,128)S(1)} custom-call(f32[128,128]{1,0:T(8,128)S(1)} %cholesky.275), custom_call_target="Cholesky" | custom-call | tf_op jit(solution)/shard_map/jit(cholesky)/cholesky | solution.py:22
  330.8 21.4 %all-gather.2.cloned.1.call-done = bf16[2048,1024]{1,0:T(8,128)(2,1)} async-done(((bf16[128,1024]{1,0:T(8,128)(2,1)}), bf16[2048,1024]{1,0:T(8,128)(2,1)}) %all-gather.2.cloned.1.call-update) | async-done | bytes 4194320 | tf_op jit(solution)/shard_map/all_gather | solution.py:44
  352.2 5.9 %convolution_convert_fusion = bf16[2048,512]{1,0:T(8,128)(2,1)} fusion(bf16[2048,1024]{1,0:T(8,128)(2,1)} %all-gather.2.cloned.1.call-done, bf16[1,512,1024]{2,1,0:T(8,128)(2,1)S(1)} %copy-done), kind=kOutput, calls=%fused_computation.2 | convolution fusion | flops 2148532224 | bytes 7340032 | tf_op jit(solution)/shard_map/dot_general | solution.py:43
  358.1 0.6 select_reduce_fusion.1
  358.8 9.8 %custom-call.32 = f32[1,128,128]{1,2,0:T(8,128)S(1)} custom-call(f32[1,128,128]{2,1,0:T(8,128)S(1)} %get-tuple-element.25), custom_call_target="InvertDiagBlocksLowerTriangular" | custom-call | tf_op jit(solution)/shard_map/jit(cholesky)/cholesky | solution.py:22
  368.6 0.8 convolution_dynamic-update-slice_fusion.1
  369.4 1.5 convolution_subtract_fusion.4
  370.9 11.9 %cholesky.255 = f32[128,128]{1,0:T(8,128)S(1)} custom-call(f32[128,128]{1,0:T(8,128)S(1)} %convolution_subtract_fusion.4), custom_call_target="Cholesky" | custom-call | tf_op jit(solution)/shard_map/jit(cholesky)/cholesky | solution.py:22
  382.8 0.6 compare_reduce_fusion.2
  384.8 0.6 compare_reduce_fusion.1
  386.1 0.6 select_reduce_fusion
  386.7 0.6 compare_reduce_fusion
  388.0 2.3 select_select_fusion
  390.3 13.6 %while.1 = (s32[]{:T(128)}, f32[512,512]{1,0:T(8,128)}, s32[4,2]{0,1:T(2,128)S(1)}, f32[4,128,128]{2,1,0:T(8,128)}, s32[]{:T(128)}) while((s32[]{:T(128)}, f32[512,512]{1,0:T(8,128)}, s32[4,2]{0,1:T(2,128)S(1)}, f32[4,128,128]{2,1,0:T(8,128)}, s32[]{:T(128)}) %tuple.35), condition=%wide.while_cond, body=%wide.while_body.sunk | while | flops 2 | bytes 132205 | solution.py:23
  390.3 0.1 constant_dynamic-slice_fusion.2
  390.4 0.5 fusion.68
  390.9 2.8 bitcast_dynamic-update-slice_fusion.2
  393.8 0.1 constant_dynamic-slice_fusion.2
  393.8 0.5 fusion.68
  394.4 2.8 bitcast_dynamic-update-slice_fusion.2
  397.2 0.1 constant_dynamic-slice_fusion.2
  397.3 0.5 fusion.68
  397.8 2.8 bitcast_dynamic-update-slice_fusion.2
  400.7 0.5 fusion.68
  401.2 2.8 bitcast_dynamic-update-slice_fusion.2
  404.0 40.1 %custom-call.33 = f32[4,128,128]{1,2,0:T(8,128)S(1)} custom-call(f32[4,128,128]{2,1,0:T(8,128)} %get-tuple-element.9), custom_call_target="InvertDiagBlocksLowerTriangular" | custom-call | tf_op jit(solution)/shard_map/triangular_solve | solution.py:23
  444.1 0.6 fusion.31
  444.8 1.5 convolution_subtract_fusion.1
  446.3 0.6 fusion.47
  446.9 1.8 convolution_subtract_fusion
  448.7 0.6 fusion.45
  449.4 0.8 copy-done.5
  450.1 2.8 fusion.7
  453.0 2.4 collective-permute-start.1
  455.4 1.7 fusion.44
  457.1 1.6 fusion.10
  458.8 1.3 copy.10
  460.1 2.6 collective-permute-done.1
  462.7 0.7 copy.32
  (37 shorter events, 0.4 us)
Async XLA Ops:
  7.2 345.0 %copy-start = (bf16[1,512,1024]{2,1,0:T(8,128)(2,1)S(1)}, bf16[1,512,1024]{2,1,0:T(8,128)(2,1)}, u32[]{:S(2)}) copy-start(bf16[1,512,1024]{2,1,0:T(8,128)(2,1)} %param.10) | copy-start | bytes 3145732
  7.2 7.4 %copy-start.9 = (bf16[1,1024,512]{2,1,0:T(8,128)(2,1)S(1)}, bf16[1,1024,512]{2,1,0:T(8,128)(2,1)}, u32[]{:S(2)}) copy-start(bf16[1,1024,512]{2,1,0:T(8,128)(2,1)} %param.11) | copy-start | bytes 3145732
  7.2 32.0 %copy-start.10 = (bf16[1,128,1024]{2,1,0:T(8,128)(2,1)S(1)}, bf16[1,128,1024]{2,1,0:T(8,128)(2,1)}, u32[]{:S(2)}) copy-start(bf16[1,128,1024]{2,1,0:T(8,128)(2,1)} %param.6) | copy-start | bytes 786436
  7.2 182.8 %all-reduce.5.cloned.1.call-start = ((), (), s32[]{:S(2)}) async-start(), calls=%async_computation.3 | async-start | bytes 4194304 | tf_op jit(solution)/shard_map/psum | solution.py:58
  8.7 5.6 %collective-permute-start = (f32[3,1024]{1,0:T(4,128)S(1)}, f32[3,1024]{1,0:T(4,128)S(1)}, u32[]{:S(2)}, u32[]{:S(2)}) collective-permute-start(f32[3,1024]{1,0:T(4,128)S(1)} %slice.150), channel_id=1, source_target_pairs={{8,0},{16,8},{24,16},{32,24},{40,32},{48,40},{56,48},{64,56},{72,6... | collective-permute-start | bytes 36872 | tf_op jit(solution)/shard_map/ppermute | solution.py:13
  14.5 26.4 %copy-start.8 = (bf16[128,1024]{1,0:T(8,128)(2,1)}, bf16[128,1024]{1,0:T(8,128)(2,1)S(1)}, u32[]{:S(2)}) copy-start(bf16[128,1024]{1,0:T(8,128)(2,1)S(1)} %fusion.22) | copy-start | bytes 786436
  41.0 227.5 %all-reduce.7.cloned.1.call-start = ((), (), s32[]{:S(2)}) async-start(), calls=%async_computation.4 | async-start | bytes 2097152 | tf_op jit(solution)/shard_map/psum | solution.py:60
  196.8 155.4 %all-gather.2.cloned.1.call-start = ((), (), s32[]{:S(2)}) async-start(), calls=%async_computation.1 | async-start | bytes 4456448 | tf_op jit(solution)/shard_map/all_gather | solution.py:44
  197.5 255.5 %reduce-scatter.2.cloned.1.call-start = ((), (), s32[]{:S(2)}) async-start(), calls=%async_computation.2 | async-start | bytes 2359296 | tf_op jit(solution)/shard_map/reduce_scatter | solution.py:49
  268.5 1.7 copy-start.6
  270.4 1.0 copy-start.7
  317.6 40.5 %copy-start.4 = (f32[512,512]{1,0:T(8,128)}, f32[512,512]{1,0:T(8,128)S(1)}, u32[]{:S(2)}) copy-start(f32[512,512]{1,0:T(8,128)S(1)} %convolution_dynamic-update-slice_fusion) | copy-start | bytes 3145732
  358.1 86.0 %copy-start.1 = (f32[1024,512]{0,1:T(8,128)S(1)}, f32[1024,512]{0,1:T(8,128)}, u32[]{:S(2)}) copy-start(f32[1024,512]{0,1:T(8,128)} %all-reduce.5.cloned.1.call-done) | copy-start | bytes 6291460
  444.8 4.6 copy-start.2
  446.9 2.4 copy-start.3
  449.3 0.8 copy-start.5
  453.0 9.7 %collective-permute-start.1 = (bf16[256,512]{1,0:T(8,128)(2,1)}, bf16[256,512]{1,0:T(8,128)(2,1)S(1)}, u32[]{:S(2)}, u32[]{:S(2)}) collective-permute-start(bf16[256,512]{1,0:T(8,128)(2,1)} %reduce-scatter.2.cloned.1.call-done), channel_id=1, source_target_pairs={{0,384},{128,0},{256,128},{384,256},{1,385},{129,1},{257,129},{385... | collective-permute-start | bytes 786440 | tf_op jit(solution)/shard_map/ppermute | solution.py:18
Sparse Core Ops, SparseCore 0:
  41.1 148.8 all-reduce.4
  196.9 71.6 all-reduce.6
  271.2 80.9 all-gather.1
  358.2 33.6 reduce-scatter.1
where the time goes:
time: 475 us; the launch traced here: 470 us
  waiting for transfers between devices  248 us (52%)
  other arithmetic  127 us (27%)
  matrix products  30.9 us (7%)
  blocking collectives  24.3 us (5%)
  local copies, waits for them, and re-layouts  19.3 us (4%)
  between operations  17 us (4%)
    psum x1, waiting for transfers between devices, local(): sketch = lax.psum(sketch_part, 'seq')  149 us
    another operation x14, other arithmetic, finish_basis(): low = jnp.linalg.cholesky(gram)  79.9 us
    psum x1, waiting for transfers between devices, local(): gram = lax.psum(gram_part, 'tensor')  70.5 us
    another operation x3, other arithmetic, finish_basis(): lax.linalg.triangular_solve(low, sketch.T, left_side=True, lower=True)  42.5 us
    psum x1, blocking collectives, local(): sketch_rows = lax.psum(row_terms, 'tensor').astype(jnp.bfloat16)  24.3 us
    all_gather x1, waiting for transfers between devices, local(): lax.all_gather(in_grad, 'seq', axis=0, tiled=True)  21.4 us
    another operation x12, local copies, waits for them, and re-layouts  13.6 us
    another operation x7, matrix products, finish_basis(): lax.linalg.triangular_solve(low, sketch.T, left_side=True, lower=True)  9.66 us
  transfers between devices with their start and end apart: 6, of which 5 were waited for; matrix products, arithmetic and copies ran while one was open for 34% of the time, Pallas kernels for 0%

commit v1 on v0

--- a/solution.py
+++ b/solution.py
@@ -3,8 +3,26 @@
 import jax.numpy as jnp
 from jax import lax
 from jax.sharding import PartitionSpec as P
+from jax.lax import axis_index, axis_size, ppermute
 
 D = 8192
+
+
+def measure_panels(link_axis, array_here, k_dim):
+    slots = axis_size(link_axis)
+    entries = tuple(((c, (c + 1) % slots) for c in range(slots)))
+    cards = tuple(((c, (c - 1) % slots) for c in range(slots)))
+    tmp, ready = ([array_here], [array_here])
+    for _ in range(slots // 2):
+        tmp.append(ppermute(tmp[-1], axis_name=link_axis, perm=entries))
+    hop_no = 0
+    while hop_no < (slots - 1) // 2:
+        ready.append(ppermute(ready[-1], axis_name=link_axis, perm=cards))
+        hop_no += 1
+    s_next = jnp.concatenate([*tmp[::-1], *ready[1:]], axis=k_dim)
+    return jnp.roll(
+        s_next, shift=(axis_index(link_axis) - slots // 2) * array_here.shape[k_dim], axis=k_dim
+    )
 
 
 def passed_along(block, axis, distance):
@@ -41,7 +59,7 @@
         total = total + kernel[tap].astype(jnp.float32) * extended[tap : tap + tok_rows]
     in_grad = total.astype(jnp.bfloat16)
     partial_grad = lax.dot_general(
-        lax.all_gather(in_grad, "seq", axis=0, tiled=True),
+        measure_panels("seq", in_grad, 0),
         weights,
         (((1,), (1,)), ((), ())),
         preferred_element_type=jnp.float32,

time: 475 us -> 528 us (1.11)
  the two profiles are of different devices: /device:TPU:26 before, /device:TPU:31 now
where the time goes in v1:
time: 528 us; the launch traced here: 521 us
  waiting for transfers between devices  198 us (38%)
  other arithmetic  129 us (24%)
  local copies, waits for them, and re-layouts  55.8 us (11%)
  starting transfers between devices  54.3 us (10%)
  matrix products  35.1 us (7%)
  blocking collectives  32.4 us (6%)
  between operations  17 us (3%)
    psum x1, waiting for transfers between devices, local(): sketch = lax.psum(sketch_part, 'seq')  103 us
    another operation x14, other arithmetic, finish_basis(): low = jnp.linalg.cholesky(gram)  80.5 us
    psum x1, waiting for transfers between devices, local(): gram = lax.psum(gram_part, 'tensor')  67.1 us
    another operation x3, other arithmetic, finish_basis(): lax.linalg.triangular_solve(low, sketch.T, left_side=True, lower=True)  42.5 us
    unnamed x49, local copies, waits for them, and re-layouts  37.8 us
    ppermute x7, starting transfers between devices, measure_panels(): ready.append(ppermute(ready[-1], axis_name=link_axis, perm=cards))  33 us
    psum x1, blocking collectives, local(): sketch_rows = lax.psum(row_terms, 'tensor').astype(jnp.bfloat16)  32.4 us
    ppermute x8, waiting for transfers between devices, measure_panels(): tmp.append(ppermute(tmp[-1], axis_name=link_axis, perm=entries))  19.2 us
  transfers between devices with their start and end apart: 20, of which 10 were waited for; matrix products, arithmetic and copies ran while one was open for 40% of the time, Pallas kernels for 0%

profile of v1, /device:TPU:31, one launch (start us, length us, event | category | flops | bytes accessed | tf_op | source)
XLA Modules:
  0.0 521.1 jit_solution(7117792824593556437)
XLA Ops:
  10.7 2.5 collective-permute-done
  13.5 3.5 collective-permute-start.1
  17.0 11.5 %collective-permute-done.1 = bf16[128,1024]{1,0:T(8,128)(2,1)S(1)} collective-permute-done((bf16[128,1024]{1,0:T(8,128)(2,1)S(1)}, bf16[128,1024]{1,0:T(8,128)(2,1)S(1)}, u32[]{:S(2)}, u32[]{:S(2)}) %collective-permute-start.1) | collective-permute-done | bytes 262176 | tf_op jit(solution)/shard_map/ppermute | solution.py:17
  28.6 1.9 collective-permute-start.2
  30.5 4.6 collective-permute-start.9
  35.1 2.3 collective-permute-done.2
  37.3 1.9 collective-permute-start.3
  39.2 4.6 collective-permute-start.10
  43.8 1.8 collective-permute-done.3
  45.6 1.9 collective-permute-start.4
  47.6 4.6 collective-permute-start.11
  52.1 1.8 collective-permute-done.4
  53.9 1.9 collective-permute-start.5
  55.9 4.6 collective-permute-start.12
  60.5 1.8 collective-permute-done.5
  62.3 1.9 collective-permute-start.6
  64.2 2.2 fusion.20
  66.4 4.6 collective-permute-start.13
  71.0 1.9 collective-permute-start.7
  72.9 32.4 %all-reduce.8 = bf16[128,512]{1,0:T(8,128)(2,1)S(1)} all-reduce(f32[128,512]{1,0:T(8,128)} %fusion.20), channel_id=1, replica_groups=mesh['pipe'=4,'seq'=16,'tensor'=8] {'tensor'}, use_global_device_ids=true, to_apply=%region_1.2 | all-reduce | flops 65536 | bytes 393216 | tf_op jit(solution)/shard_map/psum | solution.py:72
  105.4 4.9 collective-permute-start.14
  110.3 1.9 collective-permute-start.8
  112.2 2.8 convolution_bitcast_fusion
  116.4 5.3 %collective-permute-start.15 = (bf16[128,1024]{1,0:T(8,128)(2,1)}, bf16[128,1024]{1,0:T(8,128)(2,1)S(1)}, u32[]{:S(2)}, u32[]{:S(2)}) collective-permute-start(bf16[128,1024]{1,0:T(8,128)(2,1)} %collective-permute-done.14), channel_id=1, source_target_pairs={{0,120},{8,0},{16,8},{24,16},{32,24},{40,32},{48,40},{56,48},{64,5... | collective-permute-start | bytes 786440 | tf_op jit(solution)/shard_map/ppermute | solution.py:20
  121.8 1.7 constant_dynamic-update-slice_fusion.31
  123.4 1.7 constant_dynamic-update-slice_fusion.30
  125.1 1.7 constant_dynamic-update-slice_fusion.29
  133.3 1.7 constant_dynamic-update-slice_fusion.19
  135.0 1.7 constant_dynamic-update-slice_fusion.18
  136.7 1.7 constant_dynamic-update-slice_fusion.17
  139.1 1.7 constant_dynamic-update-slice_fusion.15
  140.8 1.7 constant_dynamic-update-slice_fusion.14
  142.4 1.7 constant_dynamic-update-slice_fusion.13
  148.5 103.1 %all-reduce.5.cloned.1.call-done = f32[1024,512]{0,1:T(8,128)} async-done(((f32[1024,512]{0,1:T(8,128)}), f32[1024,512]{0,1:T(8,128)}) %all-reduce.5.cloned.1.call-update) | async-done | bytes 2097168 | tf_op jit(solution)/shard_map/psum | solution.py:76
  251.6 6.7 %fusion.62 = f32[512,512]{0,1:T(8,128)} fusion(f32[1024,512]{0,1:T(8,128)} %all-reduce.5.cloned.1.call-done), kind=kOutput, calls=%fused_computation.138 | convolution fusion | flops 3221225472 | bytes 3145728 | tf_op jit(solution)/shard_map/dot_general | solution.py:77
  261.0 1.7 constant_dynamic-update-slice_fusion.3
  262.7 1.7 constant_dynamic-update-slice_fusion.2
  264.3 1.7 constant_dynamic-update-slice_fusion.1
  266.8 5.9 %fusion.2 = bf16[2048,512]{1,0:T(8,128)(2,1)} fusion(bf16[4096,1024]{1,0:T(8,128)(2,1)} %constant_dynamic-update-slice_fusion, s32[]{:T(128)S(6)} %select_n.18, bf16[1,512,1024]{2,1,0:T(8,128)(2,1)S(1)} %copy-done), kind=kOutput, calls=%fused_computation.4 | convolution fusion | flops 2148532224 | bytes 7340036 | tf_op jit(solution)/shard_map/dot_general | solution.py:61
  272.7 67.1 %all-reduce.7.cloned.1.call-done = f32[512,512]{0,1:T(8,128)} async-done(((f32[512,512]{0,1:T(8,128)}), f32[512,512]{0,1:T(8,128)}) %all-reduce.7.cloned.1.call-update) | async-done | bytes 1048592 | tf_op jit(solution)/shard_map/psum | solution.py:78
  339.8 2.5 copy.9
  342.3 1.8 fusion.19
  345.1 11.7 %cholesky.104 = f32[128,128]{1,0:T(8,128)S(1)} custom-call(f32[128,128]{1,0:T(8,128)S(1)} %cholesky.266), custom_call_target="Cholesky" | custom-call | tf_op jit(solution)/shard_map/jit(cholesky)/cholesky | solution.py:40
  357.9 9.8 %custom-call.30 = f32[1,128,128]{1,2,0:T(8,128)S(1)} custom-call(f32[1,128,128]{2,1,0:T(8,128)S(1)} %get-tuple-element.31), custom_call_target="InvertDiagBlocksLowerTriangular" | custom-call | tf_op jit(solution)/shard_map/jit(cholesky)/cholesky | solution.py:40
  367.7 1.9 constant_dynamic-update-slice_fusion.35
  370.9 11.9 %cholesky.217 = f32[128,128]{1,0:T(8,128)S(1)} custom-call(f32[128,128]{1,0:T(8,128)S(1)} %cholesky.270), custom_call_target="Cholesky" | custom-call | tf_op jit(solution)/shard_map/jit(cholesky)/cholesky | solution.py:40
  383.4 9.8 %custom-call.31 = f32[1,128,128]{1,2,0:T(8,128)S(1)} custom-call(f32[1,128,128]{2,1,0:T(8,128)S(1)} %get-tuple-element.28), custom_call_target="InvertDiagBlocksLowerTriangular" | custom-call | tf_op jit(solution)/shard_map/jit(cholesky)/cholesky | solution.py:40
  395.6 11.7 %cholesky.238 = f32[128,128]{1,0:T(8,128)S(1)} custom-call(f32[128,128]{1,0:T(8,128)S(1)} %cholesky.275), custom_call_target="Cholesky" | custom-call | tf_op jit(solution)/shard_map/jit(cholesky)/cholesky | solution.py:40
  408.0 9.8 %custom-call.32 = f32[1,128,128]{1,2,0:T(8,128)S(1)} custom-call(f32[1,128,128]{2,1,0:T(8,128)S(1)} %get-tuple-element.25), custom_call_target="InvertDiagBlocksLowerTriangular" | custom-call | tf_op jit(solution)/shard_map/jit(cholesky)/cholesky | solution.py:40
  420.0 11.9 %cholesky.255 = f32[128,128]{1,0:T(8,128)S(1)} custom-call(f32[128,128]{1,0:T(8,128)S(1)} %convolution_subtract_fusion.4), custom_call_target="Cholesky" | custom-call | tf_op jit(solution)/shard_map/jit(cholesky)/cholesky | solution.py:40
  437.0 2.3 select_select_fusion
  439.4 13.7 %while.1 = (s32[]{:T(128)}, f32[512,512]{1,0:T(8,128)}, s32[4,2]{0,1:T(2,128)S(1)}, f32[4,128,128]{2,1,0:T(8,128)}, s32[]{:T(128)}) while((s32[]{:T(128)}, f32[512,512]{1,0:T(8,128)}, s32[4,2]{0,1:T(2,128)S(1)}, f32[4,128,128]{2,1,0:T(8,128)}, s32[]{:T(128)}) %tuple.35), condition=%wide.while_cond, body=%wide.while_body.sunk | while | flops 2 | bytes 132205 | solution.py:41
  440.0 2.8 bitcast_dynamic-update-slice_fusion.2
  443.4 2.8 bitcast_dynamic-update-slice_fusion.2
  446.8 2.8 bitcast_dynamic-update-slice_fusion.2
  450.3 2.8 bitcast_dynamic-update-slice_fusion.2
  453.1 40.1 %custom-call.33 = f32[4,128,128]{1,2,0:T(8,128)S(1)} custom-call(f32[4,128,128]{2,1,0:T(8,128)} %get-tuple-element.9), custom_call_target="InvertDiagBlocksLowerTriangular" | custom-call | tf_op jit(solution)/shard_map/triangular_solve | solution.py:41
  493.8 1.5 convolution_subtract_fusion.1
  496.0 1.8 convolution_subtract_fusion
  499.2 2.8 fusion.12
  502.0 2.4 collective-permute-start.16
  504.5 1.7 fusion.49
  506.2 1.6 fusion.15
  509.1 4.5 collective-permute-done.16
  (90 shorter events, 39.3 us)
Async XLA Ops:
  7.2 259.6 %copy-start = (bf16[1,512,1024]{2,1,0:T(8,128)(2,1)S(1)}, bf16[1,512,1024]{2,1,0:T(8,128)(2,1)}, u32[]{:S(2)}) copy-start(bf16[1,512,1024]{2,1,0:T(8,128)(2,1)} %param.10) | copy-start | bytes 3145732
  7.2 244.4 %all-reduce.5.cloned.1.call-start = ((), (), s32[]{:S(2)}) async-start(), calls=%async_computation.2 | async-start | bytes 4194304 | tf_op jit(solution)/shard_map/psum | solution.py:76
  8.6 4.7 collective-permute-start
  13.5 15.1 %collective-permute-start.1 = (bf16[128,1024]{1,0:T(8,128)(2,1)S(1)}, bf16[128,1024]{1,0:T(8,128)(2,1)S(1)}, u32[]{:S(2)}, u32[]{:S(2)}) collective-permute-start(bf16[128,1024]{1,0:T(8,128)(2,1)S(1)} %fusion.27), channel_id=1, source_target_pairs={{0,8},{8,16},{16,24},{24,32},{32,40},{40,48},{48,56},{56,64},{64,7... | collective-permute-start | bytes 786440 | tf_op jit(solution)/shard_map/ppermute | solution.py:17
  28.6 8.8 %collective-permute-start.2 = (bf16[128,1024]{1,0:T(8,128)(2,1)S(1)}, bf16[128,1024]{1,0:T(8,128)(2,1)S(1)}, u32[]{:S(2)}, u32[]{:S(2)}) collective-permute-start(bf16[128,1024]{1,0:T(8,128)(2,1)S(1)} %collective-permute-done.1), channel_id=1, source_target_pairs={{0,8},{8,16},{16,24},{24,32},{32,40},{40,48},{48,56},{56,64},{64,7... | collective-permute-start | bytes 786440 | tf_op jit(solution)/shard_map/ppermute | solution.py:17
  30.5 8.8 %collective-permute-start.9 = (bf16[128,1024]{1,0:T(8,128)(2,1)S(1)}, bf16[128,1024]{1,0:T(8,128)(2,1)S(1)}, u32[]{:S(2)}, u32[]{:S(2)}) collective-permute-start(bf16[128,1024]{1,0:T(8,128)(2,1)S(1)} %fusion.27), channel_id=1, source_target_pairs={{0,120},{8,0},{16,8},{24,16},{32,24},{40,32},{48,40},{56,48},{64,5... | collective-permute-start | bytes 786440 | tf_op jit(solution)/shard_map/ppermute | solution.py:20
  37.3 8.3 %collective-permute-start.3 = (bf16[128,1024]{1,0:T(8,128)(2,1)S(1)}, bf16[128,1024]{1,0:T(8,128)(2,1)S(1)}, u32[]{:S(2)}, u32[]{:S(2)}) collective-permute-start(bf16[128,1024]{1,0:T(8,128)(2,1)S(1)} %collective-permute-done.2), channel_id=1, source_target_pairs={{0,8},{8,16},{16,24},{24,32},{32,40},{40,48},{48,56},{56,64},{64,7... | collective-permute-start | bytes 786440 | tf_op jit(solution)/shard_map/ppermute | solution.py:17
  39.2 8.3 %collective-permute-start.10 = (bf16[128,1024]{1,0:T(8,128)(2,1)S(1)}, bf16[128,1024]{1,0:T(8,128)(2,1)S(1)}, u32[]{:S(2)}, u32[]{:S(2)}) collective-permute-start(bf16[128,1024]{1,0:T(8,128)(2,1)S(1)} %collective-permute-done.9), channel_id=1, source_target_pairs={{0,120},{8,0},{16,8},{24,16},{32,24},{40,32},{48,40},{56,48},{64,5... | collective-permute-start | bytes 786440 | tf_op jit(solution)/shard_map/ppermute | solution.py:20
  45.6 8.3 %collective-permute-start.4 = (bf16[128,1024]{1,0:T(8,128)(2,1)S(1)}, bf16[128,1024]{1,0:T(8,128)(2,1)S(1)}, u32[]{:S(2)}, u32[]{:S(2)}) collective-permute-start(bf16[128,1024]{1,0:T(8,128)(2,1)S(1)} %collective-permute-done.3), channel_id=1, source_target_pairs={{0,8},{8,16},{16,24},{24,32},{32,40},{40,48},{48,56},{56,64},{64,7... | collective-permute-start | bytes 786440 | tf_op jit(solution)/shard_map/ppermute | solution.py:17
  47.6 8.4 %collective-permute-start.11 = (bf16[128,1024]{1,0:T(8,128)(2,1)S(1)}, bf16[128,1024]{1,0:T(8,128)(2,1)S(1)}, u32[]{:S(2)}, u32[]{:S(2)}) collective-permute-start(bf16[128,1024]{1,0:T(8,128)(2,1)S(1)} %collective-permute-done.10), channel_id=1, source_target_pairs={{0,120},{8,0},{16,8},{24,16},{32,24},{40,32},{48,40},{56,48},{64,5... | collective-permute-start | bytes 786440 | tf_op jit(solution)/shard_map/ppermute | solution.py:20
  53.9 8.3 %collective-permute-start.5 = (bf16[128,1024]{1,0:T(8,128)(2,1)S(1)}, bf16[128,1024]{1,0:T(8,128)(2,1)S(1)}, u32[]{:S(2)}, u32[]{:S(2)}) collective-permute-start(bf16[128,1024]{1,0:T(8,128)(2,1)S(1)} %collective-permute-done.4), channel_id=1, source_target_pairs={{0,8},{8,16},{16,24},{24,32},{32,40},{40,48},{48,56},{56,64},{64,7... | collective-permute-start | bytes 786440 | tf_op jit(solution)/shard_map/ppermute | solution.py:17
  55.9 10.5 %collective-permute-start.12 = (bf16[128,1024]{1,0:T(8,128)(2,1)S(1)}, bf16[128,1024]{1,0:T(8,128)(2,1)}, u32[]{:S(2)}, u32[]{:S(2)}) collective-permute-start(bf16[128,1024]{1,0:T(8,128)(2,1)S(1)} %collective-permute-done.11), channel_id=1, source_target_pairs={{0,120},{8,0},{16,8},{24,16},{32,24},{40,32},{48,40},{56,48},{64,5... | collective-permute-start | bytes 786440 | tf_op jit(solution)/shard_map/ppermute | solution.py:20
  62.3 8.7 %collective-permute-start.6 = (bf16[128,1024]{1,0:T(8,128)(2,1)S(1)}, bf16[128,1024]{1,0:T(8,128)(2,1)}, u32[]{:S(2)}, u32[]{:S(2)}) collective-permute-start(bf16[128,1024]{1,0:T(8,128)(2,1)S(1)} %collective-permute-done.5), channel_id=1, source_target_pairs={{0,8},{8,16},{16,24},{24,32},{32,40},{40,48},{48,56},{56,64},{64,7... | collective-permute-start | bytes 786440 | tf_op jit(solution)/shard_map/ppermute | solution.py:17
  66.4 39.0 %collective-permute-start.13 = (bf16[128,1024]{1,0:T(8,128)(2,1)}, bf16[128,1024]{1,0:T(8,128)(2,1)}, u32[]{:S(2)}, u32[]{:S(2)}) collective-permute-start(bf16[128,1024]{1,0:T(8,128)(2,1)} %collective-permute-done.12), channel_id=1, source_target_pairs={{0,120},{8,0},{16,8},{24,16},{32,24},{40,32},{48,40},{56,48},{64,5... | collective-permute-start | bytes 786440 | tf_op jit(solution)/shard_map/ppermute | solution.py:20
  71.0 39.2 %collective-permute-start.7 = (bf16[128,1024]{1,0:T(8,128)(2,1)}, bf16[128,1024]{1,0:T(8,128)(2,1)}, u32[]{:S(2)}, u32[]{:S(2)}) collective-permute-start(bf16[128,1024]{1,0:T(8,128)(2,1)} %collective-permute-done.6), channel_id=1, source_target_pairs={{0,8},{8,16},{16,24},{24,32},{32,40},{40,48},{48,56},{56,64},{64,7... | collective-permute-start | bytes 786440 | tf_op jit(solution)/shard_map/ppermute | solution.py:17
  105.4 11.1 %collective-permute-start.14 = (bf16[128,1024]{1,0:T(8,128)(2,1)}, bf16[128,1024]{1,0:T(8,128)(2,1)}, u32[]{:S(2)}, u32[]{:S(2)}) collective-permute-start(bf16[128,1024]{1,0:T(8,128)(2,1)} %collective-permute-done.13), channel_id=1, source_target_pairs={{0,120},{8,0},{16,8},{24,16},{32,24},{40,32},{48,40},{56,48},{64,5... | collective-permute-start | bytes 786440 | tf_op jit(solution)/shard_map/ppermute | solution.py:20
  110.3 11.5 %collective-permute-start.8 = (bf16[128,1024]{1,0:T(8,128)(2,1)}, bf16[128,1024]{1,0:T(8,128)(2,1)}, u32[]{:S(2)}, u32[]{:S(2)}) collective-permute-start(bf16[128,1024]{1,0:T(8,128)(2,1)} %collective-permute-done.7), channel_id=1, source_target_pairs={{0,8},{8,16},{16,24},{24,32},{32,40},{40,48},{48,56},{56,64},{64,7... | collective-permute-start | bytes 786440 | tf_op jit(solution)/shard_map/ppermute | solution.py:17
  115.0 224.7 %all-reduce.7.cloned.1.call-start = ((), (), s32[]{:S(2)}) async-start(), calls=%async_computation.3 | async-start | bytes 2097152 | tf_op jit(solution)/shard_map/psum | solution.py:78
  116.4 21.9 %collective-permute-start.15 = (bf16[128,1024]{1,0:T(8,128)(2,1)}, bf16[128,1024]{1,0:T(8,128)(2,1)S(1)}, u32[]{:S(2)}, u32[]{:S(2)}) collective-permute-start(bf16[128,1024]{1,0:T(8,128)(2,1)} %collective-permute-done.14), channel_id=1, source_target_pairs={{0,120},{8,0},{16,8},{24,16},{32,24},{40,32},{48,40},{56,48},{64,5... | collective-permute-start | bytes 786440 | tf_op jit(solution)/shard_map/ppermute | solution.py:20
  138.3 9.5 %copy-start.6 = (bf16[128,1024]{1,0:T(8,128)(2,1)}, bf16[128,1024]{1,0:T(8,128)(2,1)S(1)}, u32[]{:S(2)}) copy-start(bf16[128,1024]{1,0:T(8,128)(2,1)S(1)} %collective-permute-done.15) | copy-start | bytes 786436
  148.5 117.5 %copy-start.7 = (bf16[128,1024]{1,0:T(8,128)(2,1)S(1)}, bf16[128,1024]{1,0:T(8,128)(2,1)}, u32[]{:S(2)}) copy-start(bf16[128,1024]{1,0:T(8,128)(2,1)} %copy-done.6) | copy-start | bytes 786436
  258.3 243.8 %reduce-scatter.2.cloned.1.call-start = ((), (), s32[]{:S(2)}) async-start(), calls=%async_computation.1 | async-start | bytes 2359296 | tf_op jit(solution)/shard_map/reduce_scatter | solution.py:67
  272.7 220.5 %copy-start.1 = (f32[1024,512]{0,1:T(8,128)S(1)}, f32[1024,512]{0,1:T(8,128)}, u32[]{:S(2)}) copy-start(f32[1024,512]{0,1:T(8,128)} %all-reduce.5.cloned.1.call-done) | copy-start | bytes 6291460
  344.1 1.0 copy-start.5
  493.8 4.6 copy-start.2
  496.0 2.4 copy-start.3
  498.4 0.8 copy-start.4
  502.0 11.6 %collective-permute-start.16 = (bf16[256,512]{1,0:T(8,128)(2,1)}, bf16[256,512]{1,0:T(8,128)(2,1)S(1)}, u32[]{:S(2)}, u32[]{:S(2)}) collective-permute-start(bf16[256,512]{1,0:T(8,128)(2,1)} %reduce-scatter.2.cloned.1.call-done), channel_id=1, source_target_pairs={{0,384},{128,0},{256,128},{384,256},{1,385},{129,1},{257,129},{385... | collective-permute-start | bytes 786440 | tf_op jit(solution)/shard_map/ppermute | solution.py:36
Sparse Core Ops, SparseCore 0:
  115.2 136.3 all-reduce.4
  258.4 81.3 all-reduce.6
  342.6 40.2 reduce-scatter.1
